TPU v7x, 128 devices: a whole 4x4x4 slice. The times are simulated.
128 devices in a mesh: seq: 16 (over x, y), grp: 8 (over z, core).
Axes of the slice: x: 4, y: 4, z: 4, core: 2. Of those that a mesh axis runs over, the one named last changes fastest.
Arguments:
- video: bfloat16 [65536, 1536], P(('grp', 'seq')), parts along dimension 0, may hold values from -28 to 28
- audio: bfloat16 [8192, 1536], P(('grp', 'seq')), parts along dimension 0, may hold values from -28 to 28
- wq_video: bfloat16 [1536, 1536], replicated, may hold values from -0.3125 to 0.3125
- wk_video: bfloat16 [1536, 1536], replicated, may hold values from -0.15625 to 0.15625
- wv_video: bfloat16 [1536, 1536], replicated, may hold values from -0.15625 to 0.15625
- wo_video: bfloat16 [1536, 1536], replicated, may hold values from -0.875 to 0.875
- wq_audio: bfloat16 [1536, 1536], P('seq'), may hold values from -0.3125 to 0.3125
- wk_audio: bfloat16 [1536, 1536], P('seq'), may hold values from -0.15625 to 0.15625
- wv_audio: bfloat16 [1536, 1536], P('seq'), may hold values from -0.15625 to 0.15625
- wo_audio: bfloat16 [1536, 1536], P('seq'), may hold values from -0.875 to 0.875
Outputs:
- video_out: bfloat16 [65536, 1536], P(('grp', 'seq')), parts along dimension 0
- audio_out: bfloat16 [8192, 1536], P(('grp', 'seq')), parts along dimension 0
There are 8 independent parts, one for each index of `grp`. A program takes and returns all parts, laid end to end along the dimension named above; an argument that names none is the same for every part. Nothing has to cross between parts.
All inputs are finite; a program needn't handle non-finite values.
Results may differ from a plain program's by a relative error of at most 0.035.
The roundings to bfloat16 on the way count: a program that leaves them out, or rounds other values in their place, can miss the bound.
Values may be sent and summed in bfloat16 or wider, within the bound.
A program may use at most 192 MiB of HBM per device.

v0:
```python
import jax
import jax.numpy as jnp
from jax import lax
from jax.sharding import PartitionSpec as P

HEADS = 12
HEAD_DIM = 128


def by_heads(rows):
    return rows.reshape(rows.shape[0], HEADS, HEAD_DIM)


def project(rows, weight):
    return jnp.dot(rows, weight, preferred_element_type=jnp.float32).astype(jnp.bfloat16)


def on_device(
    video, audio, wq_video, wk_video, wv_video, wo_video, wq_audio, wk_audio, wv_audio, wo_audio
):
    temper = HEAD_DIM ** (-0.5)
    inner = HEADS * HEAD_DIM
    aq_weight, ak_weight, av_weight, ao_weight = (
        lax.all_gather(wq_audio, "seq", axis=0, tiled=True),
        lax.all_gather(wk_audio, "seq", axis=0, tiled=True),
        lax.all_gather(wv_audio, "seq", axis=0, tiled=True),
        lax.all_gather(wo_audio, "seq", axis=0, tiled=True),
    )
    q_video = project(video, wq_video)
    k_video = project(video, wk_video)
    v_video = project(video, wv_video)
    own_q = project(audio, aq_weight)
    own_k = project(audio, ak_weight)
    own_v = project(audio, av_weight)
    all_q, all_k, all_v = (
        lax.all_gather(own_q, "seq", axis=0, tiled=True),
        lax.all_gather(own_k, "seq", axis=0, tiled=True),
        lax.all_gather(own_v, "seq", axis=0, tiled=True),
    )
    scores = (
        jnp.einsum(
            "qhd,khd->hqk", by_heads(q_video), by_heads(all_k), preferred_element_type=jnp.float32
        )
        * temper
    )
    peak = jnp.max(scores, axis=-1, keepdims=True)
    expo_front = jnp.exp(scores - peak)
    sums = jnp.sum(expo_front, axis=-1)
    weights = expo_front.astype(jnp.bfloat16)
    blended = jnp.einsum(
        "hqk,khd->qhd", weights, by_heads(all_v), preferred_element_type=jnp.float32
    )
    attended = (blended / jnp.transpose(sums)[:, :, None]).astype(jnp.bfloat16)
    video_out = project(attended.reshape(video.shape[0], inner), wo_video)
    back_scores = (
        jnp.einsum(
            "qhd,khd->hqk", by_heads(all_q), by_heads(k_video), preferred_element_type=jnp.float32
        )
        * temper
    )
    peak_back = jnp.max(back_scores, axis=-1)
    expo_back = jnp.exp(back_scores - peak_back[:, :, None])
    totals = jnp.sum(expo_back, axis=-1)
    numerator = jnp.einsum(
        "hqk,khd->qhd",
        expo_back.astype(jnp.bfloat16),
        by_heads(v_video),
        preferred_element_type=jnp.float32,
    )
    audio_rows = all_q.shape[0]
    global_peak = lax.pmax(peak_back.astype(jnp.bfloat16), "seq").astype(peak_back.dtype)
    factor = jnp.exp(peak_back - global_peak)
    scaled_numer = (numerator * jnp.transpose(factor)[:, :, None]).reshape(audio_rows, inner)
    scaled_total = jnp.transpose(totals * factor)
    own_numer, own_total = (
        lax.psum_scatter(
            scaled_numer.astype(jnp.bfloat16), "seq", scatter_dimension=0, tiled=True
        ).astype(jnp.float32),
        lax.psum_scatter(
            scaled_total.astype(jnp.bfloat16), "seq", scatter_dimension=0, tiled=True
        ).astype(jnp.float32),
    )
    merged = by_heads(own_numer) / own_total[:, :, None]
    audio_attended = merged.astype(jnp.bfloat16).reshape(audio.shape[0], inner)
    audio_out = project(audio_attended, ao_weight)
    return (video_out, audio_out)


def solution(mesh):
    in_specs = (
        P(("grp", "seq"), None),
        P(("grp", "seq"), None),
        P(),
        P(),
        P(),
        P(),
        P("seq", None),
        P("seq", None),
        P("seq", None),
        P("seq", None),
    )
    out_specs = (P(("grp", "seq"), None), P(("grp", "seq"), None))
    return jax.shard_map(
        on_device, mesh=mesh, in_specs=in_specs, out_specs=out_specs, check_vma=False
    )
```

profile of v0, /device:TPU:1, one launch (start us, length us, event | category | flops | bytes accessed | tf_op | source)
XLA Modules:
  0.0 546.1 jit_solution(12590477874941387528)
XLA Ops:
  7.2 0.0 copy-start
  7.2 0.0 copy-start.3
  7.2 0.0 all-gather.16.cloned.1.call-start
  7.2 0.7 all-gather.16.cloned.1.call-update
  7.9 0.0 all-gather.12.cloned.1.call-start
  8.0 0.7 all-gather.12.cloned.1.call-update
  8.7 0.0 all-gather.8.cloned.1.call-start
  8.7 0.7 all-gather.8.cloned.1.call-update
  9.4 0.0 all-gather.18.cloned.1.call-start
  9.5 57.9 %all-gather.16.cloned.1.call-done = bf16[1536,1536]{1,0:T(8,128)(2,1)} async-done(((bf16[96,1536]{1,0:T(8,128)(2,1)}), bf16[1536,1536]{1,0:T(8,128)(2,1)}) %all-gather.16.cloned.1.call-update) | async-done | bytes 4718608 | tf_op jit(solution)/shard_map/all_gather | solution.py:24
  67.3 4.1 convolution_convert_fusion.5
  71.4 0.0 all-gather.18.cloned.1.call-update
  71.4 0.0 all-gather.14.cloned.1.call-start
  71.5 51.7 %all-gather.12.cloned.1.call-done = bf16[1536,1536]{1,0:T(8,128)(2,1)} async-done(((bf16[96,1536]{1,0:T(8,128)(2,1)}), bf16[1536,1536]{1,0:T(8,128)(2,1)}) %all-gather.12.cloned.1.call-update) | async-done | bytes 4718608 | tf_op jit(solution)/shard_map/all_gather | solution.py:25
  123.2 0.0 copy-done.3
  123.2 3.9 convolution_convert_fusion.6
  127.1 0.0 all-gather.14.cloned.1.call-update
  127.1 0.0 all-gather.10.cloned.1.call-start
  127.2 51.8 %all-gather.8.cloned.1.call-done = bf16[1536,1536]{1,0:T(8,128)(2,1)} async-done(((bf16[96,1536]{1,0:T(8,128)(2,1)}), bf16[1536,1536]{1,0:T(8,128)(2,1)}) %all-gather.8.cloned.1.call-update) | async-done | bytes 4718608 | tf_op jit(solution)/shard_map/all_gather | solution.py:26
  179.0 3.9 convolution_convert_fusion.7
  182.9 0.0 all-gather.10.cloned.1.call-update
  182.9 0.0 reduce-scatter.9.cloned.1.call-start
  183.0 0.0 copy-done
  183.0 4.9 convolution_convert_fusion
  187.9 1.6 copy.37
  189.5 6.2 %convolution_convert_fusion.1 = bf16[512,1536]{1,0:T(8,128)(2,1)} fusion(bf16[512,1536]{1,0:T(8,128)(2,1)S(1)} %copy-done, bf16[1536,1536]{1,0:T(8,128)(2,1)} %param.14), kind=kOutput, calls=%fused_computation.19 | convolution fusion | flops 2416705536 | bytes 7864320 | tf_op jit(solution)/shard_map/dot_general | solution.py:15
  195.7 1.7 copy.35
  197.4 30.9 %all-gather.18.cloned.1.call-done = bf16[1024,1536]{1,0:T(8,128)(2,1)} async-done(((bf16[64,1536]{1,0:T(8,128)(2,1)}), bf16[1024,1536]{1,0:T(8,128)(2,1)}) %all-gather.18.cloned.1.call-update) | async-done | bytes 3145744 | tf_op jit(solution)/shard_map/all_gather | solution.py:36
  228.3 4.7 copy.36
  233.0 14.4 %multiply_reduce_fusion = (f32[12,1024]{1,0:T(8,128)S(1)}, f32[12,1024,512]{1,2,0:T(8,128)}) fusion(bf16[1024,12,128]{0,2,1:T(8,128)(2,1)} %bitcast.51, bf16[512,12,128]{0,2,1:T(8,128)(2,1)} %bitcast.54), kind=kOutput, calls=%fused_computation.2 | convolution fusion | flops 1623183360 | bytes 29933568 | tf_op jit(solution)/shard_map/qhd,khd->hqk/dot_general | solution.py:56
  247.4 58.5 %pmax.7 = bf16[12,1024]{1,0:T(8,128)(2,1)S(1)} all-reduce(bf16[12,1024]{1,0:T(8,128)(2,1)S(1)} %convert_element_type.71), channel_id=1, replica_groups=mesh['seq'=16,'grp'=8] {'seq'}, use_global_device_ids=true, to_apply=%region_3.0 | all-reduce | flops 12288 | bytes 49152 | tf_op jit(solution)/shard_map/pmax | solution.py:71
  305.8 10.6 %fusion.2 = f32[12,1024]{1,0:T(8,128)S(1)} fusion(f32[12,1024,512]{1,2,0:T(8,128)} %get-tuple-element.7, f32[12,1024]{1,0:T(8,128)S(1)} %get-tuple-element.6), kind=kLoop, calls=%fused_computation.6 | loop fusion | flops 18862080 | bytes 25264128 | tf_op jit(solution)/shard_map/reduce_sum | solution.py:63
  316.5 0.9 copy.48
  317.4 0.0 reduce-scatter.9.cloned.1.call-update
  317.4 0.2 reduce-scatter.7.cloned.1.call-start
  317.6 12.4 %fusion.12 = bf16[1024,12,128]{0,2,1:T(8,128)(2,1)} fusion(f32[1024,12]{0,1:T(8,128)S(1)} %get-tuple-element.3, bf16[512,12,128]{0,2,1:T(8,128)(2,1)S(1)} %bitcast.53, f32[12,1024,512]{1,2,0:T(8,128)} %get-tuple-element.7, f32[12,1024]{1,0:T(8,128)S(1)} %get-tuple-element.6), kind=kOutput, calls=%fused_computation.15 | convolution fusion | flops 1632632832 | bytes 29982720 | tf_op jit(solution)/shard_map/hqk,khd->qhd/dot_general | solution.py:64
  330.1 4.7 copy.46
  334.7 0.0 reduce-scatter.7.cloned.1.call-update
  334.7 0.0 all-gather.20.cloned.1.call-start
  334.8 0.7 all-gather.20.cloned.1.call-update
  335.5 4.9 convolution_convert_fusion.3
  340.4 0.7 copy.31
  341.1 0.0 all-gather.14.cloned.1.call-done
  341.2 4.7 copy.32
  345.8 0.0 all-gather.10.cloned.1.call-done
  345.8 4.7 copy.30
  350.5 12.2 %multiply_reduce_fusion.1 = (f32[12,512]{1,0:T(8,128)S(1)}, f32[12,512,1024]{2,1,0:T(8,128)}) fusion(bf16[512,12,128]{0,2,1:T(8,128)(2,1)S(1)} %bitcast.50, bf16[1024,12,128]{0,2,1:T(8,128)(2,1)} %bitcast.49), kind=kOutput, calls=%fused_computation.3 | convolution fusion | flops 1623189504 | bytes 29908992 | tf_op jit(solution)/shard_map/qhd,khd->hqk/dot_general | solution.py:41
  362.7 0.0 copy-start.2
  362.7 11.3 %fusion = f32[12,512]{1,0:T(8,128)S(1)} fusion(f32[12,512,1024]{2,1,0:T(8,128)} %get-tuple-element.5, f32[12,512]{1,0:T(8,128)S(1)} %get-tuple-element.4), kind=kLoop, calls=%fused_computation.4 | loop fusion | flops 18868224 | bytes 25214976 | tf_op jit(solution)/shard_map/reduce_sum | solution.py:48
  374.1 0.0 copy-done.2
  374.1 10.9 %fusion.13 = bf16[512,12,128]{0,2,1:T(8,128)(2,1)S(1)} fusion(bf16[1024,12,128]{0,2,1:T(8,128)(2,1)S(1)} %bitcast.55, f32[12,512,1024]{2,1,0:T(8,128)} %get-tuple-element.5, f32[12,512]{1,0:T(8,128)S(1)} %get-tuple-element.4, f32[512,12]{0,1:T(8,128)S(1)} %bitcast.56), kind=kOutput, calls=%fused_computation.17 | convolution fusion | flops 1631059968 | bytes 29933568 | tf_op jit(solution)/shard_map/hqk,khd->qhd/dot_general | solution.py:50
  385.0 0.0 copy-start.1
  385.0 6.2 %convolution_convert_fusion.2 = bf16[512,1536]{1,0:T(8,128)(2,1)} fusion(bf16[512,1536]{0,1:T(8,128)(2,1)S(1)} %bitcast.57, bf16[1536,1536]{1,0:T(8,128)(2,1)} %param.15), kind=kOutput, calls=%fused_computation.20 | convolution fusion | flops 2416705536 | bytes 7864320 | tf_op jit(solution)/shard_map/dot_general | solution.py:15
  391.2 8.3 %reduce-scatter.9.cloned.1.call-done = bf16[64,12]{1,0:T(8,128)(2,1)} async-done(((bf16[1024,12]{1,0:T(8,128)(2,1)}), bf16[64,12]{1,0:T(8,128)(2,1)}) %reduce-scatter.9.cloned.1.call-update) | async-done | bytes 1552
  399.5 0.8 copy.49
  400.3 77.9 %reduce-scatter.7.cloned.1.call-done = bf16[64,1536]{1,0:T(8,128)(2,1)} async-done(((bf16[1024,1536]{1,0:T(8,128)(2,1)}), bf16[64,1536]{1,0:T(8,128)(2,1)}) %reduce-scatter.7.cloned.1.call-update) | async-done | bytes 196624
  478.2 1.1 copy.47
  479.4 0.1 fusion.18
  479.5 56.1 %all-gather.20.cloned.1.call-done = bf16[1536,1536]{1,0:T(8,128)(2,1)} async-done(((bf16[96,1536]{1,0:T(8,128)(2,1)}), bf16[1536,1536]{1,0:T(8,128)(2,1)}) %all-gather.20.cloned.1.call-update) | async-done | bytes 4718608 | tf_op jit(solution)/shard_map/all_gather | solution.py:27
  535.6 4.0 convolution_convert_fusion.4
  539.5 0.0 copy-done.1
  (3 shorter events, 0.0 us)
Async XLA Ops:
  7.2 175.8 %copy-start = (bf16[512,1536]{1,0:T(8,128)(2,1)S(1)}, bf16[512,1536]{1,0:T(8,128)(2,1)}, u32[]{:S(2)}) copy-start(bf16[512,1536]{1,0:T(8,128)(2,1)} %param.10) | copy-start | bytes 4718596
  7.2 116.0 %copy-start.3 = (bf16[64,1536]{1,0:T(8,128)(2,1)S(1)}, bf16[64,1536]{1,0:T(8,128)(2,1)}, u32[]{:S(2)}) copy-start(bf16[64,1536]{1,0:T(8,128)(2,1)} %param.11) | copy-start | bytes 589828
  7.2 60.1 %all-gather.16.cloned.1.call-start = ((), (), s32[]{:S(2)}) async-start(), calls=%async_computation.6 | async-start | bytes 5013504 | tf_op jit(solution)/shard_map/all_gather | solution.py:24
  7.9 115.2 %all-gather.12.cloned.1.call-start = ((), (), s32[]{:S(2)}) async-start(), calls=%async_computation.4 | async-start | bytes 5013504 | tf_op jit(solution)/shard_map/all_gather | solution.py:25
  8.7 170.3 %all-gather.8.cloned.1.call-start = ((), (), s32[]{:S(2)}) async-start(), calls=%async_computation.2 | async-start | bytes 5013504 | tf_op jit(solution)/shard_map/all_gather | solution.py:26
  9.4 218.9 %all-gather.18.cloned.1.call-start = ((), (), s32[]{:S(2)}) async-start(), calls=%async_computation.7 | async-start | bytes 3342336 | tf_op jit(solution)/shard_map/all_gather | solution.py:36
  71.4 269.7 %all-gather.14.cloned.1.call-start = ((), (), s32[]{:S(2)}) async-start(), calls=%async_computation.5 | async-start | bytes 3342336 | tf_op jit(solution)/shard_map/all_gather | solution.py:37
  127.1 218.7 %all-gather.10.cloned.1.call-start = ((), (), s32[]{:S(2)}) async-start(), calls=%async_computation.3 | async-start | bytes 3342336 | tf_op jit(solution)/shard_map/all_gather | solution.py:38
  182.9 216.6 %reduce-scatter.9.cloned.1.call-start = ((), (), s32[]{:S(2)}) async-start(), calls=%async_computation.10 | async-start | bytes 278528
  317.4 160.8 %reduce-scatter.7.cloned.1.call-start = ((), (), s32[]{:S(2)}) async-start(), calls=%async_computation.9 | async-start | bytes 3342336
  334.7 200.8 %all-gather.20.cloned.1.call-start = ((), (), s32[]{:S(2)}) async-start(), calls=%async_computation.8 | async-start | bytes 5013504 | tf_op jit(solution)/shard_map/all_gather | solution.py:27
  362.7 11.3 %copy-start.2 = (bf16[1024,1536]{0,1:T(8,128)(2,1)S(1)}, bf16[1024,1536]{0,1:T(8,128)(2,1)}, u32[]{:S(2)}) copy-start(bf16[1024,1536]{0,1:T(8,128)(2,1)} %copy.30) | copy-start | bytes 9437188
  385.0 154.6 %copy-start.1 = (bf16[512,1536]{1,0:T(8,128)(2,1)S(1)}, bf16[512,1536]{1,0:T(8,128)(2,1)}, u32[]{:S(2)}) copy-start(bf16[512,1536]{1,0:T(8,128)(2,1)} %param.10) | copy-start | bytes 4718596
Sparse Core Ops, SparseCore 0:
  10.2 57.0 all-gather.15
  69.5 53.5 all-gather.11
  125.3 53.5 all-gather.7
  181.0 47.2 all-gather.17
  230.3 46.9 all-gather.13
  279.9 46.7 all-gather.9
  329.9 69.5 reduce-scatter.8
  403.2 74.9 reduce-scatter.6
  480.7 54.8 all-gather.19
where the time goes:
time: 547 us; the launch traced here: 546 us
  waiting for transfers between devices  337 us (62%)
  matrix products  88 us (16%)
  blocking collectives  58.5 us (11%)
  local copies, waits for them, and re-layouts  25.6 us (5%)
  other arithmetic  22.1 us (4%)
  between operations  14 us (3%)
    unnamed x11, waiting for transfers between devices  89.1 us
    pmax x1, blocking collectives, on_device(): lax.pmax(peak_back.astype(jnp.bfloat16), 'seq').astype(peak_back.dtype)  58.5 us
    all_gather x1, waiting for transfers between devices, on_device(): lax.all_gather(wq_audio, 'seq', axis=0, tiled=True)  57.9 us
    all_gather x1, waiting for transfers between devices, on_device(): lax.all_gather(wo_audio, 'seq', axis=0, tiled=True)  56.1 us
    all_gather x1, waiting for transfers between devices, on_device(): lax.all_gather(wv_audio, 'seq', axis=0, tiled=True)  51.8 us
    all_gather x1, waiting for transfers between devices, on_device(): lax.all_gather(wk_audio, 'seq', axis=0, tiled=True)  51.7 us
    dot_general x8, matrix products, project(): jnp.dot(rows, weight, preferred_element_type=jnp.float32)  38.1 us
    all_gather x1, waiting for transfers between devices, on_device(): lax.all_gather(own_q, 'seq', axis=0, tiled=True)  30.9 us
  transfers between devices with their start and end apart: 9, of which 7 were waited for; matrix products, arithmetic and copies ran while one was open for 24% of the time, Pallas kernels for 0%

commit v1 on v0

v1 whole, which is shorter than its diff:
```python
import functools

import jax
import jax.numpy as jnp
from jax import lax
from jax.experimental import pallas as pl
from jax.experimental.pallas import tpu as pltpu
from jax.sharding import PartitionSpec as P

HEADS = 12
HEAD_DIM = 128
D = 1536
INNER = 1536
ROWS = 512
OWN = 64
PART = 384
STRIPE = 48
MESH = pl.DeviceIdType.MESH
F32 = jnp.float32
BF16 = jnp.bfloat16
ANY = pl.BlockSpec(memory_space=pl.ANY)


def place():
    s, g = lax.axis_index("seq"), lax.axis_index("grp")
    return s // 4, s % 4, g // 2, g % 2


def device(x, y, z, c):
    return (x * 4 + y, z * 2 + c)


def remote(src, dst, send, recv, to):
    return pltpu.make_async_remote_copy(
        src_ref=src, dst_ref=dst, send_sem=send, recv_sem=recv, device_id=to, device_id_type=MESH
    )


class Sems:
    def __init__(self, send, recv, local):
        self.send, self.recv, self.local = send, recv, local
        self.n_remote, self.n_local = 0, 0

    def remote(self, src, dst, to):
        i = self.n_remote
        self.n_remote += 1
        return remote(src, dst, self.send.at[i], self.recv.at[i], to)

    def copy(self, src, dst):
        i = self.n_local
        self.n_local += 1
        return pltpu.make_async_copy(src, dst, self.local.at[i])


def start(copies):
    for copy in copies:
        copy.start()
    return copies


def arrived(copies):
    for copy in copies:
        copy.wait_recv()


def left(copies):
    for copy in copies:
        copy.wait_send()


def greet(devices):
    barrier = pltpu.get_barrier_semaphore()
    for to in devices:
        pl.semaphore_signal(barrier, inc=1, device_id=to, device_id_type=MESH)
    pl.semaphore_wait(barrier, len(devices))


def gather_first(sems, buf, x, y, z, c):
    half = INNER // 2
    xr = x % 2
    pair = device(x + 1 - 2 * xr, y, z, c)
    ones = [sems.remote(buf.at[xr, y, c, :, :half], buf.at[xr, y, c, :, :half], pair)]
    twos = []
    for dy in (1, 3, 2):
        part = buf.at[xr, y, c, :, half:]
        twos.append(sems.remote(part, part, device(x, (y + dy) % 4, z, c)))
    return start(ones + twos)


def gather_second(sems, buf, x, y, z, c):
    half = INNER // 2
    xr = x % 2
    pair = device(x + 1 - 2 * xr, y, z, c)
    copies = []
    for dy in (1, 3, 2):
        part = buf.at[:, y, c, :, :half]
        copies.append(sems.remote(part, part, device(x, (y + dy) % 4, z, c)))
    part = buf.at[xr, :, c, :, half:]
    copies.append(sems.remote(part, part, pair))
    return start(copies)


def gather_third(sems, buf, x, y, z, c):
    part = buf.at[:, :, c]
    return start([sems.remote(part, part, device(x, y, z, 1 - c))])


def k1(
    video, audio, wq, wk, wv, aqw, akw, avw, aow,
    qo, ko, vo, gqo, owno, woo,
    wcol, arows, vid, wbuf, pres, gq, own, proj,
    send, recv, local,
):
    x, y, z, c = place()
    s = x * 4 + y
    xr = x % 2
    native = c == x // 2
    xd = jnp.where(native, x, 3 - x)
    cd = jnp.where(native, c, 1 - c)
    partner = device(3 - x, y, z, 1 - c)
    sibling = device(x, y, z, 1 - c)
    sems = Sems(send, recv, local)

    stripes = [
        sems.copy(
            w.at[pl.ds(pl.multiple_of(c * STRIPE, 16), STRIPE), pl.ds(pl.multiple_of(z * PART, 128), PART)],
            wcol.at[x, y, c, :, i * PART : (i + 1) * PART],
        )
        for i, w in enumerate((aqw, akw, avw, aow))
    ]
    own_audio = sems.copy(audio, arows.at[z])
    weights = [sems.copy(w, wbuf.at[i]) for i, w in enumerate((wq, wk, wv))]
    own_video = sems.copy(video, vid)
    start(stripes + [own_audio])

    xs = [device((x + d) % 4, y, z, c) for d in (1, 3, 2)]
    ys = [device(x, (y + d) % 4, z, c) for d in (1, 3, 2)]
    zs = [device(x, y, (z + d) % 4, c) for d in (1, 3, 2)]
    cross = [device(3 - x, y, (z + d) % 4, 1 - c) for d in range(4)]
    greet(xs + ys + zs + cross + [sibling])

    first, second, last = slice(0, 512), slice(512, 1152), slice(1152, 1536)
    for copy in stripes:
        copy.wait()
    mine = wcol.at[x, y, c]
    a_x = start([sems.remote(mine.at[:, first], mine.at[:, first], to) for to in xs])
    a_y = start([sems.remote(mine.at[:, second], mine.at[:, second], to) for to in ys])
    own_audio.wait()
    a_z = start([sems.remote(arows.at[z], arows.at[z], to) for to in zs])
    swap = sems.remote(video, vid, partner)
    pl.when(native)(own_video.start)
    pl.when(jnp.logical_not(native))(swap.start)
    start(weights)
    arrived(a_x)
    part = wcol.at[:, y, c, :, first]
    b_y = start([sems.remote(part, part, to) for to in ys])
    arrived(a_y)
    part = wcol.at[x, :, c, :, second]
    b_x = start([sems.remote(part, part, to) for to in xs])
    arrived(b_y)
    part = wcol.at[:, :, c, :, first]
    c_1 = start([sems.remote(part, part, sibling)])
    arrived(b_x)
    part = wcol.at[:, :, c, :, second]
    c_2 = start([sems.remote(part, part, sibling)])
    arrived(a_z)
    arrived(c_1)

    rows = arows[...].reshape(4 * OWN, D)
    to_owner = []
    slot_x = xd % 2
    for i in range(3):
        if i == 1:
            arrived(c_2)
        cols = slice(i * PART, (i + 1) * PART)
        weight = wcol[:, :, :, :, cols].reshape(D, PART)
        pres[i] = jnp.dot(rows, weight, preferred_element_type=F32).astype(BF16).reshape(4, OWN, PART)
        lanes = pl.ds(pl.multiple_of(z * PART, 128), PART)
        target = gq.at[slot_x, y, cd, :, lanes] if i == 0 else own.at[i - 1, :, lanes]
        group = []
        for dz in range(1, 4):
            zd = (z + dz) % 4
            group.append(sems.remote(pres.at[i, zd], target, device(xd, y, zd, cd)))
        start(group)
        here = sems.copy(pres.at[i, z], target)
        away = sems.remote(pres.at[i, z], target, device(xd, y, z, cd))
        pl.when(native)(here.start)
        pl.when(jnp.logical_not(native))(away.start)
        to_owner.append((group, here, away))

    def landed(i):
        group, here, away = to_owner[i]
        arrived(group)
        pl.when(native)(here.wait)
        pl.when(jnp.logical_not(native))(away.wait_recv)

    o_x = start([sems.remote(mine.at[:, last], mine.at[:, last], to) for to in xs])

    def project(i):
        weights[i].wait()

        @pl.loop(0, INNER // 256)
        def _(n):
            lanes = pl.ds(pl.multiple_of(n * 256, 256), 256)
            proj[i, :, lanes] = jnp.dot(vid[...], wbuf[i, :, lanes], preferred_element_type=F32).astype(BF16)

    landed(0)
    g_1 = gather_first(sems, gq, x, y, z, c)
    pl.when(native)(own_video.wait)
    pl.when(jnp.logical_not(native))(swap.wait_recv)
    project(0)
    outs = [sems.copy(proj.at[i], o) for i, o in enumerate((qo, ko, vo))]
    outs[0].start()
    arrived(g_1)
    g_2 = gather_second(sems, gq, x, y, z, c)
    arrived(o_x)
    part = wcol.at[:, y, c, :, last]
    o_y = start([sems.remote(part, part, to) for to in ys])
    project(1)
    outs[1].start()
    arrived(g_2)
    g_3 = gather_third(sems, gq, x, y, z, c)
    project(2)
    outs[2].start()
    landed(1)
    landed(2)
    own_out = sems.copy(own, owno)
    own_out.start()
    arrived(o_y)
    o_out = sems.copy(wcol.at[:, :, c, :, last], woo)
    o_out.start()
    arrived(g_3)
    q_out = sems.copy(gq, gqo)
    q_out.start()
    left(a_x + a_y + a_z + b_x + b_y + c_1 + c_2 + o_x + o_y + g_1 + g_2 + g_3)
    for group, here, away in to_owner:
        left(group)
        pl.when(jnp.logical_not(native))(away.wait_send)
    pl.when(jnp.logical_not(native))(swap.wait_send)
    for copy in outs + [own_out, o_out, q_out]:
        copy.wait()


def call_k1(*args):
    sds = jax.ShapeDtypeStruct
    return pl.pallas_call(
        k1,
        out_shape=[sds((ROWS, INNER), BF16)] * 3
        + [sds((2, 4, 2, OWN, INNER), BF16), sds((2, OWN, INNER), BF16), sds((4, 4, STRIPE, PART), BF16)],
        in_specs=[ANY] * 9,
        out_specs=[ANY] * 6,
        scratch_shapes=[
            pltpu.VMEM((4, 4, 2, STRIPE, 4 * PART), BF16),
            pltpu.VMEM((4, OWN, D), BF16),
            pltpu.VMEM((ROWS, D), BF16),
            pltpu.VMEM((3, D, INNER), BF16),
            pltpu.VMEM((3, 4, OWN, PART), BF16),
            pltpu.VMEM((2, 4, 2, OWN, INNER), BF16),
            pltpu.VMEM((2, OWN, INNER), BF16),
            pltpu.VMEM((3, ROWS, INNER), BF16),
            pltpu.SemaphoreType.DMA((64,)),
            pltpu.SemaphoreType.DMA((64,)),
            pltpu.SemaphoreType.DMA((32,)),
        ],
        compiler_params=pltpu.CompilerParams(collective_id=1, has_side_effects=True, vmem_limit_bytes=56 * 2**20),
        name="project_and_gather",
    )(*args)


SCALE = HEAD_DIM**-0.5 * 1.4426950408889634
HALF = INNER // 2


def lanes_of(h):
    return pl.ds(pl.multiple_of(h * HEAD_DIM, HEAD_DIM), HEAD_DIM)


def soft(q, k, v):
    s = lax.dot_general(q, k, (((1,), (1,)), ((), ())), preferred_element_type=F32)
    m = jnp.max(s, axis=-1, keepdims=True)
    p = jnp.exp2((s - m) * SCALE)
    t = jnp.sum(p, axis=-1, keepdims=True)
    n = jnp.dot(p.astype(BF16), v, preferred_element_type=F32)
    return (n / t).astype(BF16), m, t


def merge(dst, logs_dst, srcs, logs, first_head):
    ls = [l[...] for l in logs]
    peak = functools.reduce(jnp.maximum, ls)
    ws = [jnp.exp2(l - peak) for l in ls]
    total = functools.reduce(jnp.add, ws)
    if logs_dst is not None:
        logs_dst[...] = peak + jnp.log2(total)
    ws = [w / total for w in ws]
    for i in range(dst.shape[-1] // HEAD_DIM):
        cols = slice(i * HEAD_DIM, (i + 1) * HEAD_DIM)
        h = first_head + i
        parts = [w[:, h : h + 1] * s[:, cols].astype(F32) for w, s in zip(ws, srcs)]
        dst[:, cols] = functools.reduce(jnp.add, parts).astype(BF16)


def k2(
    qi, ki, vi, gqi, owni, wo, woc,
    video_out, audio_out,
    qkv, gq, gk, gv, wov, woa, nb, logs, ra, rla, rb1, rlb1, rb2, rlb2, lmb1, lmb2, rc1, rlc1, rc2, rlc2,
    aud, att, out, aout,
    send, recv, local,
):
    x, y, z, c = place()
    xr = x % 2
    native = c == x // 2
    partner = device(3 - x, y, z, 1 - c)
    sibling = device(x, y, z, 1 - c)
    pair = device(x + 1 - 2 * xr, y, z, c)
    ys = [device(x, (y + d) % 4, z, c) for d in (1, 3, 2)]
    zs = [device(x, y, (z + d) % 4, c) for d in (1, 3, 2)]
    sems = Sems(send, recv, local)

    own_k = sems.copy(owni.at[0], gk.at[xr, y, c])
    own_v = sems.copy(owni.at[1], gv.at[xr, y, c])
    q_in = sems.copy(gqi, gq)
    ins = [sems.copy(a, qkv.at[i]) for i, a in enumerate((qi, ki, vi))]
    wo_in = sems.copy(wo, wov)
    woc_in = sems.copy(woc, woa.at[z, :, :, c])
    start([own_k, own_v, q_in, ins[1], ins[2], woc_in, ins[0], wo_in])
    greet(ys + zs + [pair, sibling, partner])

    own_k.wait()
    k_1 = gather_first(sems, gk, x, y, z, c)
    own_v.wait()
    v_1 = gather_first(sems, gv, x, y, z, c)
    woc_in.wait()
    part = woa.at[z, :, :, c]
    o_z = start([sems.remote(part, part, to) for to in zs])
    logs[...] = jnp.zeros_like(logs)
    q_in.wait()
    ins[1].wait()
    ins[2].wait()

    def back(first, last):
        @pl.loop(first, last)
        def _(h):
            cols = lanes_of(h)
            k, v = qkv[1, :, cols], qkv[2, :, cols]
            for i in range(2):
                q = gq[i, :, :, :, cols].reshape(512, HEAD_DIM)
                n, m, t = soft(q, k, v)
                nb[i, :, :, :, cols] = n.reshape(4, 2, OWN, HEAD_DIM)
                l = (m * SCALE + jnp.log2(t)).reshape(4, 2, OWN, 1)
                lane = lax.broadcasted_iota(jnp.int32, (4, 2, OWN, 128), 3)
                logs[i] = jnp.where(lane == h, l, logs[i])

    back(0, 3)
    arrived(k_1)
    k_2 = gather_second(sems, gk, x, y, z, c)
    back(3, 6)
    arrived(v_1)
    v_2 = gather_second(sems, gv, x, y, z, c)
    back(6, 9)
    arrived(k_2)
    k_3 = gather_third(sems, gk, x, y, z, c)
    back(9, 12)
    arrived(v_2)
    v_3 = gather_third(sems, gv, x, y, z, c)

    r_a = start(
        [sems.remote(nb.at[:, :, 1 - c], ra, sibling), sems.remote(logs.at[:, :, 1 - c], rla, sibling)]
    )
    ins[0].wait()
    arrived(k_3)
    arrived(v_3)
    backs = []

    def front(first, last):
        @pl.loop(first, last)
        def _(h):
            cols = lanes_of(h)
            k = gk[:, :, :, :, cols].reshape(1024, HEAD_DIM)
            v = gv[:, :, :, :, cols].reshape(1024, HEAD_DIM)
            for i in range(2):
                rows = slice(i * 256, (i + 1) * 256)
                n, _, _ = soft(qkv[0, rows, cols], k, v)
                att[0, rows, cols] = n

        cols = slice(first * HEAD_DIM, last * HEAD_DIM)
        copy = sems.remote(att.at[0, :, cols], att.at[1, :, cols], partner)
        pl.when(jnp.logical_not(native))(copy.start)
        backs.append(copy)

    front(0, 3)
    arrived(r_a)

    @pl.loop(0, 8)
    def _(b):
        i, j = b // 4, b % 4
        mine, mine_l = nb.at[i, j, c], logs.at[i, j, c]
        merge(mine, mine_l, [mine, ra.at[i, j]], [mine_l, rla.at[i, j]], 0)

    r_b1 = start(
        [
            sems.remote(nb.at[1 - xr, :, c, :, :HALF], rb1, pair),
            sems.remote(logs.at[1 - xr, :, c], rlb1, pair),
        ]
    )
    r_b2 = []
    for i, d in enumerate((1, 3, 2)):
        yd = (y + d) % 4
        r_b2.append(sems.remote(nb.at[:, yd, c, :, HALF:], rb2.at[i], ys[i]))
        r_b2.append(sems.remote(logs.at[:, yd, c], rlb2.at[i], ys[i]))
    start(r_b2)
    front(3, 6)
    arrived(r_b1)
    arrived(r_b2)

    @pl.loop(0, 4)
    def _(j):
        mine = nb.at[xr, j, c, :, :HALF]
        merge(mine, lmb1.at[j], [mine, rb1.at[j]], [logs.at[xr, j, c], rlb1.at[j]], 0)

    @pl.loop(0, 2)
    def _(i):
        mine = nb.at[i, y, c, :, HALF:]
        merge(
            mine,
            lmb2.at[i],
            [mine] + [rb2.at[d, i] for d in range(3)],
            [logs.at[i, y, c]] + [rlb2.at[d, i] for d in range(3)],
            6,
        )

    r_c = []
    for i, d in enumerate((1, 3, 2)):
        yd = (y + d) % 4
        r_c.append(sems.remote(nb.at[xr, yd, c, :, :HALF], rc1.at[i], ys[i]))
        r_c.append(sems.remote(lmb1.at[yd], rlc1.at[i], ys[i]))
    r_c.append(sems.remote(nb.at[1 - xr, y, c, :, HALF:], rc2, pair))
    r_c.append(sems.remote(lmb2.at[1 - xr], rlc2, pair))
    start(r_c)
    front(6, 9)
    arrived(r_c)
    mine = nb.at[xr, y, c, :, :HALF]
    merge(
        aud.at[0, :, :HALF],
        None,
        [mine] + [rc1.at[d] for d in range(3)],
        [lmb1.at[y]] + [rlc1.at[d] for d in range(3)],
        0,
    )
    mine = nb.at[xr, y, c, :, HALF:]
    merge(aud.at[0, :, HALF:], None, [mine, rc2], [lmb2.at[xr], rlc2], 6)
    r_d = sems.remote(aud.at[0], aud.at[1], partner)
    pl.when(jnp.logical_not(native))(r_d.start)
    arrived(o_z)
    part = woa.at[:, :, :, c]
    o_c = start([sems.remote(part, part, sibling)])
    front(9, 12)

    which = jnp.where(native, 0, 1)
    pl.when(jnp.logical_not(native))(r_d.wait_recv)
    arrived(o_c)
    rows = aud[which]
    for i in range(4):
        weight = woa[i].reshape(D, PART)
        aout[:, i * PART : (i + 1) * PART] = jnp.dot(rows, weight, preferred_element_type=F32).astype(BF16)
    a_out = sems.copy(aout, audio_out)
    a_out.start()
    wo_in.wait()
    for copy in backs:
        pl.when(jnp.logical_not(native))(copy.wait_recv)
    v_out = []

    for n in range(6):
        cols = slice(n * 256, (n + 1) * 256)
        out[:, cols] = jnp.dot(att[which], wov[:, cols], preferred_element_type=F32).astype(BF16)
        copy = sems.copy(out.at[:, cols], video_out.at[:, cols])
        copy.start()
        v_out.append(copy)

    left(k_1 + k_2 + k_3 + v_1 + v_2 + v_3 + o_z + o_c + r_a + r_b1 + r_b2 + r_c)
    for copy in backs + [r_d]:
        pl.when(jnp.logical_not(native))(copy.wait_send)
    a_out.wait()
    for copy in v_out:
        copy.wait()


def call_k2(*args):
    sds = jax.ShapeDtypeStruct
    block = (2, 4, 2, OWN, INNER)
    return pl.pallas_call(
        k2,
        out_shape=[sds((ROWS, D), BF16), sds((OWN, D), BF16)],
        in_specs=[ANY] * 7,
        out_specs=[ANY] * 2,
        scratch_shapes=[
            pltpu.VMEM((3, ROWS, INNER), BF16),
            pltpu.VMEM(block, BF16),
            pltpu.VMEM(block, BF16),
            pltpu.VMEM(block, BF16),
            pltpu.VMEM((INNER, D), BF16),
            pltpu.VMEM((4, 4, 4, 2, STRIPE, PART), BF16),
            pltpu.VMEM(block, BF16),
            pltpu.VMEM((2, 4, 2, OWN, 128), F32),
            pltpu.VMEM((2, 4, OWN, INNER), BF16),
            pltpu.VMEM((2, 4, OWN, 128), F32),
            pltpu.VMEM((4, OWN, HALF), BF16),
            pltpu.VMEM((4, OWN, 128), F32),
            pltpu.VMEM((3, 2, OWN, HALF), BF16),
            pltpu.VMEM((3, 2, OWN, 128), F32),
            pltpu.VMEM((4, OWN, 128), F32),
            pltpu.VMEM((2, OWN, 128), F32),
            pltpu.VMEM((3, OWN, HALF), BF16),
            pltpu.VMEM((3, OWN, 128), F32),
            pltpu.VMEM((OWN, HALF), BF16),
            pltpu.VMEM((OWN, 128), F32),
            pltpu.VMEM((2, OWN, INNER), BF16),
            pltpu.VMEM((2, ROWS, INNER), BF16),
            pltpu.VMEM((ROWS, D), BF16),
            pltpu.VMEM((OWN, D), BF16),
            pltpu.SemaphoreType.DMA((64,)),
            pltpu.SemaphoreType.DMA((64,)),
            pltpu.SemaphoreType.DMA((32,)),
        ],
        compiler_params=pltpu.CompilerParams(collective_id=2, has_side_effects=True, vmem_limit_bytes=60 * 2**20),
        name="attend_and_merge",
    )(*args)


def on_device(
    video, audio, wq_video, wk_video, wv_video, wo_video, wq_audio, wk_audio, wv_audio, wo_audio
):
    q, k, v, gq, own, woc = call_k1(
        video, audio, wq_video, wk_video, wv_video, wq_audio, wk_audio, wv_audio, wo_audio
    )
    return tuple(call_k2(q, k, v, gq, own, wo_video, woc))


def solution(mesh):
    tokens, rows = P(("grp", "seq"), None), P("seq", None)
    in_specs = (tokens, tokens, P(), P(), P(), P(), rows, rows, rows, rows)
    return jax.shard_map(
        on_device, mesh=mesh, in_specs=in_specs, out_specs=(tokens, tokens), check_vma=False
    )
```

time: 547 us -> 153 us (0.28)
  waiting for transfers between devices: 337 us -> 0 us
  Pallas kernels: 0 us -> 149 us
  matrix products: 88 us -> 0 us
  blocking collectives: 58.5 us -> 0 us
  local copies, waits for them, and re-layouts: 25.6 us -> 3.37 us
  other arithmetic: 22.1 us -> 0 us
  between operations: 14 us -> 0.66 us
    all_gather x7 -> x0, waiting for transfers between devices: 248 us -> none  [the longest x1 57.9 us: on_device(): lax.all_gather(wq_audio, 'seq', axis=0, tiled=True)]
    pallas_call x0 -> x2, Pallas kernels: none -> 149 us  [the longest x1 80.6 us: call_k2(): pl.pallas_call(k2, out_shape=[sds((ROWS, D), BF16), sds((OWN, D), BF16)],...]
    unnamed x11 -> x0, waiting for transfers between devices: 89.1 us -> none
    dot_general x12 -> x0, matrix products: 88 us -> none  [the longest x8 38.1 us: project(): jnp.dot(rows, weight, preferred_element_type=jnp.float32)]
    pmax x1 -> x0, blocking collectives: 58.5 us -> none  [on_device(): lax.pmax(peak_back.astype(jnp.bfloat16), 'seq').astype(peak_back.dtype)]
    reduce_sum x2 -> x0, other arithmetic: 21.9 us -> none  [the longest x1 11.3 us: on_device(): sums = jnp.sum(expo_front, axis=-1)]
    all_gather x3 -> x0, local copies, waits for them, and re-layouts: 14.1 us -> none  [the longest x1 4.73 us: on_device(): lax.all_gather(own_q, 'seq', axis=0, tiled=True)]
  transfers between devices with their start and end apart: 9 -> 0, of which waited for: 7 -> 0; matrix products, arithmetic and copies ran while one was open for 24% -> 0% of each run, Pallas kernels for 0% -> 0%
where the time goes in v1:
time: 153 us
  Pallas kernels  149 us (97%)
  local copies, waits for them, and re-layouts  3.37 us (2%)
    pallas_call x1, Pallas kernels, call_k2(): pl.pallas_call(k2, out_shape=[sds((ROWS, D), BF16), sds((OWN, D), BF16)],...  80.6 us
    pallas_call x1, Pallas kernels, call_k1(): pl.pallas_call(k1, out_shape=[sds((ROWS, INNER), BF16)] * 3 + [sds((2, 4,...  68.8 us
    unnamed x4, local copies, waits for them, and re-layouts  3.37 us

profile of v1, /device:TPU:1, one launch (start us, length us, event | category | flops | bytes accessed | tf_op | source)
XLA Modules:
  0.0 153.4 jit_solution(8602738518432046393)
XLA Ops:
  0.6 68.8 %project_and_gather.1 = (bf16[512,1536]{1,0:T(8,128)(2,1)}, bf16[512,1536]{1,0:T(8,128)(2,1)}, bf16[512,1536]{1,0:T(8,128)(2,1)}, bf16[2,4,2,64,1536]{4,3,2,1,0:...) custom-call(bf16[512,1536]{1,0:T(8,128)(2,1)} %video.1, bf16[64,1536]{1,0:T(8,128)(2,1)} %audio.1, ...), custom_call_target="tpu_custom_call" | custom-call | tf_op jit(solution)/shard_map/project_and_gather/pallas_call | solution.py:246
  69.4 80.6 %attend_and_merge.1 = (bf16[512,1536]{1,0:T(8,128)(2,1)}, bf16[64,1536]{1,0:T(8,128)(2,1)}) custom-call(bf16[512,1536]{1,0:T(8,128)(2,1)} %get-tuple-element.8.qi, bf16[512,1536]{1,0:T(8,128)(2,1)} %get-tuple-element.9.ki, bf16[512,1536]{1,0:T(8,128)(2,1)} %get-tuple-element.10.vi, bf16[2,4,2,64,1536]{4,3,2,1,0:T(8,128)(2,1)} %get-tuple-element.11.gqi, ...), custom_call_target="tpu_custom_call" | custom-call | tf_op jit(solution)/shard_map/attend_and_merge/pallas_call | solution.py:490
  150.0 0.0 copy-start
  150.0 2.7 %copy.14 = bf16[512,1536]{1,0:T(8,128)(2,1)} copy(bf16[512,1536]{1,0:T(8,128)(2,1)} %get-tuple-element.16) | data formatting | bytes 3145728
  152.7 0.0 copy-done
  152.7 0.7 copy.15
Async XLA Ops:
  150.0 2.7 %copy-start = (bf16[64,1536]{1,0:T(8,128)(2,1)S(1)}, bf16[64,1536]{1,0:T(8,128)(2,1)}, u32[]{:S(2)}) copy-start(bf16[64,1536]{1,0:T(8,128)(2,1)} %get-tuple-element.17) | copy-start | bytes 589828

commit v2 on v0

v2 whole, which is shorter than its diff:
```python
import functools

import jax
import jax.numpy as jnp
from jax import lax
from jax.experimental import pallas as pl
from jax.experimental.pallas import tpu as pltpu
from jax.sharding import PartitionSpec as P

HEADS = 12
HEAD_DIM = 128
D = 1536
INNER = 1536
ROWS = 512
OWN = 64
PART = 384
STRIPE = 48
MESH = pl.DeviceIdType.MESH
F32 = jnp.float32
BF16 = jnp.bfloat16
ANY = pl.BlockSpec(memory_space=pl.ANY)


def place():
    s, g = lax.axis_index("seq"), lax.axis_index("grp")
    return s // 4, s % 4, g // 2, g % 2


def device(x, y, z, c):
    return (x * 4 + y, z * 2 + c)


def remote(src, dst, send, recv, to):
    return pltpu.make_async_remote_copy(
        src_ref=src, dst_ref=dst, send_sem=send, recv_sem=recv, device_id=to, device_id_type=MESH
    )


class Sems:
    def __init__(self, send, recv, local):
        self.send, self.recv, self.local = send, recv, local
        self.n_remote, self.n_local = 0, 0

    def remote(self, src, dst, to):
        i = self.n_remote
        self.n_remote += 1
        return remote(src, dst, self.send.at[i], self.recv.at[i], to)

    def copy(self, src, dst):
        i = self.n_local
        self.n_local += 1
        return pltpu.make_async_copy(src, dst, self.local.at[i])


def start(copies):
    for copy in copies:
        copy.start()
    return copies


def arrived(copies):
    for copy in copies:
        copy.wait_recv()


def left(copies):
    for copy in copies:
        copy.wait_send()


def greet(devices):
    barrier = pltpu.get_barrier_semaphore()
    for to in devices:
        pl.semaphore_signal(barrier, inc=1, device_id=to, device_id_type=MESH)
    pl.semaphore_wait(barrier, len(devices))


def gather_first(sems, buf, x, y, z, c):
    half = INNER // 2
    xr = x % 2
    pair = device(x + 1 - 2 * xr, y, z, c)
    ones = [sems.remote(buf.at[xr, y, c, :, :half], buf.at[xr, y, c, :, :half], pair)]
    twos = []
    for dy in (1, 3, 2):
        part = buf.at[xr, y, c, :, half:]
        twos.append(sems.remote(part, part, device(x, (y + dy) % 4, z, c)))
    return ones + twos


def gather_second(sems, buf, x, y, z, c):
    half = INNER // 2
    xr = x % 2
    pair = device(x + 1 - 2 * xr, y, z, c)
    copies = []
    for dy in (1, 3, 2):
        part = buf.at[:, y, c, :, :half]
        copies.append(sems.remote(part, part, device(x, (y + dy) % 4, z, c)))
    part = buf.at[xr, :, c, :, half:]
    copies.append(sems.remote(part, part, pair))
    return copies


def gather_third(sems, buf, x, y, z, c):
    part = buf.at[:, :, c]
    return [sems.remote(part, part, device(x, y, z, 1 - c))]


SCALE = HEAD_DIM**-0.5 * 1.4426950408889634
HALF = INNER // 2


def lanes_of(h):
    return pl.ds(pl.multiple_of(h * HEAD_DIM, HEAD_DIM), HEAD_DIM)


def soft(q, k, v):
    s = lax.dot_general(q, k, (((1,), (1,)), ((), ())), preferred_element_type=F32)
    m = jnp.max(s, axis=-1, keepdims=True)
    p = jnp.exp2((s - m) * SCALE)
    t = jnp.sum(p, axis=-1, keepdims=True)
    n = jnp.dot(p.astype(BF16), v, preferred_element_type=F32)
    return (n / t).astype(BF16), m, t


def merge(dst, logs_dst, srcs, logs, first_head):
    ls = [l[...] for l in logs]
    peak = functools.reduce(jnp.maximum, ls)
    ws = [jnp.exp2(l - peak) for l in ls]
    total = functools.reduce(jnp.add, ws)
    if logs_dst is not None:
        logs_dst[...] = peak + jnp.log2(total)
    ws = [w / total for w in ws]
    for i in range(dst.shape[-1] // HEAD_DIM):
        cols = slice(i * HEAD_DIM, (i + 1) * HEAD_DIM)
        h = first_head + i
        parts = [w[:, h : h + 1] * s[:, cols].astype(F32) for w, s in zip(ws, srcs)]
        dst[:, cols] = functools.reduce(jnp.add, parts).astype(BF16)


def attend(
    video, audio, wq, wk, wv, wo, aqw, akw, avw, aow,
    video_out, audio_out,
    wcol, arows, vid, wbuf, pres, gq, gk, gv, qkv, woa, nb, logs, ra, rla, rb1, rlb1, rb2, rlb2,
    lmb1, lmb2, rc1, rlc1, rc2, rlc2, aud, att, out, aout,
    send, recv, local,
):
    x, y, z, c = place()
    xr = x % 2
    native = c == x // 2
    guest = jnp.logical_not(native)
    xd = jnp.where(native, x, 3 - x)
    cd = jnp.where(native, c, 1 - c)
    partner = device(3 - x, y, z, 1 - c)
    sibling = device(x, y, z, 1 - c)
    pair = device(x + 1 - 2 * xr, y, z, c)
    xs = [device((x + d) % 4, y, z, c) for d in (1, 3, 2)]
    ys = [device(x, (y + d) % 4, z, c) for d in (1, 3, 2)]
    zs = [device(x, y, (z + d) % 4, c) for d in (1, 3, 2)]
    cross = [device(3 - x, y, (z + d) % 4, 1 - c) for d in range(4)]
    sems = Sems(send, recv, local)
    sent = []

    def push(copies):
        sent.extend(copies)
        return start(copies)

    stripes = [
        sems.copy(
            w.at[pl.ds(pl.multiple_of(c * STRIPE, 16), STRIPE), pl.ds(pl.multiple_of(z * PART, 128), PART)],
            wcol.at[x, y, c, :, i * PART : (i + 1) * PART],
        )
        for i, w in enumerate((aqw, akw, avw, aow))
    ]
    own_audio = sems.copy(audio, arows.at[z])
    weights = [sems.copy(w, wbuf.at[i]) for i, w in enumerate((wq, wk, wv))]
    halves = [slice(0, ROWS // 2), slice(ROWS // 2, ROWS)]
    own_video = [sems.copy(video.at[r], vid.at[r]) for r in halves]
    start(stripes + [own_audio])
    greet(xs + ys + zs + cross + [sibling])

    mine = wcol.at[x, y, c]

    def spread_first(cols, along):
        return push([sems.remote(mine.at[:, cols], mine.at[:, cols], to) for to in along])

    def spread_x_then(cols):
        part = wcol.at[:, y, c, :, cols]
        return push([sems.remote(part, part, to) for to in ys])

    def spread_y_then(cols):
        part = wcol.at[x, :, c, :, cols]
        return push([sems.remote(part, part, to) for to in xs])

    def spread_third(cols):
        part = wcol.at[:, :, c, :, cols]
        return push([sems.remote(part, part, sibling)])

    q_a, q_b, k_a, v_a, o_a = slice(0, 256), slice(256, 384), slice(384, 768), slice(768, 1152), slice(1152, 1536)
    for copy in stripes:
        copy.wait()
    sqa = spread_first(q_a, xs)
    sqb = spread_first(q_b, ys)
    own_audio.wait()
    a_z = push([sems.remote(arows.at[z], arows.at[z], to) for to in zs])
    sk = spread_first(k_a, xs)
    sv = spread_first(v_a, ys)
    start([weights[1], weights[2], weights[0]])

    @pl.when(native)
    def _():
        start(own_video)

    arrived(sqa)
    sqa = spread_x_then(q_a)
    arrived(sqb)
    sqb = spread_y_then(q_b)
    arrived(sk)
    sk = spread_x_then(k_a)
    arrived(sv)
    sv = spread_y_then(v_a)
    logs[...] = jnp.zeros_like(logs)
    arrived(sqa + sqb)
    sq = spread_third(slice(0, 384))
    swap = [sems.remote(video.at[r], vid.at[r], partner) for r in halves]

    @pl.when(guest)
    def _():
        start(swap)

    arrived(a_z)

    slot_x = xd % 2
    to_owner = []

    def project_audio(i, buf):
        rows = arows[...].reshape(4 * OWN, D)
        weight = wcol[:, :, :, :, i * PART : (i + 1) * PART].reshape(D, PART)
        pres[i] = jnp.dot(rows, weight, preferred_element_type=F32).astype(BF16).reshape(4, OWN, PART)
        target = buf.at[slot_x, y, cd, :, pl.ds(pl.multiple_of(z * PART, 128), PART)]
        group = push(
            [sems.remote(pres.at[i, (z + d) % 4], target, device(xd, y, (z + d) % 4, cd)) for d in (1, 2, 3)]
        )
        here = sems.copy(pres.at[i, z], target)
        away = sems.remote(pres.at[i, z], target, device(xd, y, z, cd))
        pl.when(native)(here.start)
        pl.when(guest)(away.start)
        to_owner.append((group, here, away))

    def landed(i):
        group, here, away = to_owner[i]
        arrived(group)
        pl.when(native)(here.wait)
        pl.when(guest)(away.wait_recv)

    arrived(sq)
    project_audio(0, gq)
    arrived(sk)
    sk = spread_third(k_a)
    arrived(sv)
    sv = spread_third(v_a)
    landed(0)
    q_1 = push(gather_first(sems, gq, x, y, z, c))
    arrived(sk)
    project_audio(1, gk)
    arrived(sv)
    project_audio(2, gv)

    def project(i, r):
        @pl.loop(0, INNER // 256)
        def _(n):
            lanes = pl.ds(pl.multiple_of(n * 256, 256), 256)
            qkv[i, halves[r], lanes] = jnp.dot(
                vid[halves[r], :], wbuf[i, :, lanes], preferred_element_type=F32
            ).astype(BF16)

    def video_half(r):
        pl.when(native)(own_video[r].wait)
        pl.when(guest)(swap[r].wait_recv)

    weights[1].wait()
    video_half(0)
    project(1, 0)
    arrived(q_1)
    q_2 = push(gather_second(sems, gq, x, y, z, c))
    landed(1)
    k_1 = push(gather_first(sems, gk, x, y, z, c))
    weights[2].wait()
    project(2, 0)
    landed(2)
    v_1 = push(gather_first(sems, gv, x, y, z, c))
    weights[0].wait()
    project(0, 0)
    so = spread_first(o_a, xs)
    arrived(q_2)
    q_3 = push(gather_third(sems, gq, x, y, z, c))
    arrived(k_1)
    k_2 = push(gather_second(sems, gk, x, y, z, c))
    video_half(1)
    project(0, 1)
    wo_in = sems.copy(wo, wbuf.at[0])
    wo_in.start()
    project(1, 1)
    arrived(v_1)
    v_2 = push(gather_second(sems, gv, x, y, z, c))
    arrived(so)
    so = spread_x_then(o_a)
    project(2, 1)
    arrived(q_3)

    def back(first, last):
        @pl.loop(first, last)
        def _(h):
            cols = lanes_of(h)
            k, v = qkv[1, :, cols], qkv[2, :, cols]
            half = first // 6
            for i in range(2):
                q = gq[i, :, :, :, cols].reshape(512, HEAD_DIM)
                n, m, t = soft(q, k, v)
                nb[i, :, :, :, cols] = n.reshape(4, 2, OWN, HEAD_DIM)
                l = (m * SCALE + jnp.log2(t)).reshape(4, 2, OWN, 1)
                lane = lax.broadcasted_iota(jnp.int32, (4, 2, OWN, 128), 3)
                logs[half, i] = jnp.where(lane == h, l, logs[half, i])

    def to_sibling(half):
        cols = slice(half * HALF, (half + 1) * HALF)
        return push(
            [
                sems.remote(nb.at[:, :, 1 - c, :, cols], ra.at[:, :, :, cols], sibling),
                sems.remote(logs.at[half, :, :, 1 - c], rla.at[half], sibling),
            ]
        )

    def merge_sibling(half):
        cols = slice(half * HALF, (half + 1) * HALF)

        @pl.loop(0, 8)
        def _(b):
            i, j = b // 4, b % 4
            part, part_l = nb.at[i, j, c, :, cols], logs.at[half, i, j, c]
            merge(part, part_l, [part, ra.at[i, j, :, cols]], [part_l, rla.at[half, i, j]], half * 6)

    def front(first, last):
        @pl.loop(first, last)
        def _(h):
            cols = lanes_of(h)
            k = gk[:, :, :, :, cols].reshape(1024, HEAD_DIM)
            v = gv[:, :, :, :, cols].reshape(1024, HEAD_DIM)
            for i in range(2):
                n, _, _ = soft(qkv[0, halves[i], cols], k, v)
                att[0, halves[i], cols] = n

        cols = slice(first * HEAD_DIM, last * HEAD_DIM)
        copy = sems.remote(att.at[0, :, cols], att.at[1, :, cols], partner)
        pl.when(guest)(copy.start)
        return copy

    back(0, 3)
    arrived(k_2)
    k_3 = push(gather_third(sems, gk, x, y, z, c))
    back(3, 6)
    r_a1 = to_sibling(0)
    arrived(so)
    o_part = woa.at[z, :, :, c]
    o_own = sems.copy(wcol.at[:, :, c, :, o_a], o_part)
    o_own.start()
    arrived(v_2)
    v_3 = push(gather_third(sems, gv, x, y, z, c))
    o_own.wait()
    o_z = push([sems.remote(o_part, o_part, to) for to in zs])
    back(6, 9)
    arrived(r_a1)
    merge_sibling(0)
    r_b1 = push(
        [
            sems.remote(nb.at[1 - xr, :, c, :, :HALF], rb1, pair),
            sems.remote(logs.at[0, 1 - xr, :, c], rlb1, pair),
        ]
    )
    back(9, 12)
    r_a2 = to_sibling(1)
    arrived(k_3)
    arrived(v_3)
    backs = [front(0, 3)]
    arrived(r_a2)
    merge_sibling(1)
    r_b2 = []
    for i, d in enumerate((1, 3, 2)):
        yd = (y + d) % 4
        r_b2.append(sems.remote(nb.at[:, yd, c, :, HALF:], rb2.at[i], ys[i]))
        r_b2.append(sems.remote(logs.at[1, :, yd, c], rlb2.at[i], ys[i]))
    push(r_b2)
    arrived(r_b1)

    @pl.loop(0, 4)
    def _(j):
        part = nb.at[xr, j, c, :, :HALF]
        merge(part, lmb1.at[j], [part, rb1.at[j]], [logs.at[0, xr, j, c], rlb1.at[j]], 0)

    r_c1 = []
    for i, d in enumerate((1, 3, 2)):
        yd = (y + d) % 4
        r_c1.append(sems.remote(nb.at[xr, yd, c, :, :HALF], rc1.at[i], ys[i]))
        r_c1.append(sems.remote(lmb1.at[yd], rlc1.at[i], ys[i]))
    push(r_c1)
    backs.append(front(3, 6))
    arrived(r_b2)

    @pl.loop(0, 2)
    def _(i):
        part = nb.at[i, y, c, :, HALF:]
        merge(
            part,
            lmb2.at[i],
            [part] + [rb2.at[d, i] for d in range(3)],
            [logs.at[1, i, y, c]] + [rlb2.at[d, i] for d in range(3)],
            6,
        )

    r_c2 = push(
        [
            sems.remote(nb.at[1 - xr, y, c, :, HALF:], rc2, pair),
            sems.remote(lmb2.at[1 - xr], rlc2, pair),
        ]
    )
    backs.append(front(6, 9))
    arrived(r_c1)
    merge(
        aud.at[0, :, :HALF],
        None,
        [nb.at[xr, y, c, :, :HALF]] + [rc1.at[d] for d in range(3)],
        [lmb1.at[y]] + [rlc1.at[d] for d in range(3)],
        0,
    )
    arrived(r_c2)
    merge(aud.at[0, :, HALF:], None, [nb.at[xr, y, c, :, HALF:], rc2], [lmb2.at[xr], rlc2], 6)
    r_d = sems.remote(aud.at[0], aud.at[1], partner)
    pl.when(guest)(r_d.start)
    arrived(o_z)
    part = woa.at[:, :, :, c]
    o_c = push([sems.remote(part, part, sibling)])
    backs.append(front(9, 12))

    which = jnp.where(native, 0, 1)
    pl.when(guest)(r_d.wait_recv)
    arrived(o_c)
    rows = aud[which]
    for i in range(4):
        weight = woa[i].reshape(D, PART)
        aout[:, i * PART : (i + 1) * PART] = jnp.dot(rows, weight, preferred_element_type=F32).astype(BF16)
    a_out = sems.copy(aout, audio_out)
    a_out.start()
    wo_in.wait()
    for copy in backs:
        pl.when(guest)(copy.wait_recv)
    v_out = []
    for n in range(6):
        cols = slice(n * 256, (n + 1) * 256)
        out[:, cols] = jnp.dot(att[which], wbuf[0, :, cols], preferred_element_type=F32).astype(BF16)
        copy = sems.copy(out.at[:, cols], video_out.at[:, cols])
        copy.start()
        v_out.append(copy)

    left(sent)

    @pl.when(guest)
    def _():
        left(swap + backs + [r_d] + [away for _, _, away in to_owner])

    a_out.wait()
    for copy in v_out:
        copy.wait()


def on_device(*args):
    sds = jax.ShapeDtypeStruct
    block = (2, 4, 2, OWN, INNER)
    return tuple(
        pl.pallas_call(
            attend,
            out_shape=[sds((ROWS, D), BF16), sds((OWN, D), BF16)],
            in_specs=[ANY] * 10,
            out_specs=[ANY] * 2,
            scratch_shapes=[
                pltpu.VMEM((4, 4, 2, STRIPE, 4 * PART), BF16),
                pltpu.VMEM((4, OWN, D), BF16),
                pltpu.VMEM((ROWS, D), BF16),
                pltpu.VMEM((3, D, INNER), BF16),
                pltpu.VMEM((3, 4, OWN, PART), BF16),
                pltpu.VMEM(block, BF16),
                pltpu.VMEM(block, BF16),
                pltpu.VMEM(block, BF16),
                pltpu.VMEM((3, ROWS, INNER), BF16),
                pltpu.VMEM((4, 4, 4, 2, STRIPE, PART), BF16),
                pltpu.VMEM(block, BF16),
                pltpu.VMEM((2, 2, 4, 2, OWN, 128), F32),
                pltpu.VMEM((2, 4, OWN, INNER), BF16),
                pltpu.VMEM((2, 2, 4, OWN, 128), F32),
                pltpu.VMEM((4, OWN, HALF), BF16),
                pltpu.VMEM((4, OWN, 128), F32),
                pltpu.VMEM((3, 2, OWN, HALF), BF16),
                pltpu.VMEM((3, 2, OWN, 128), F32),
                pltpu.VMEM((4, OWN, 128), F32),
                pltpu.VMEM((2, OWN, 128), F32),
                pltpu.VMEM((3, OWN, HALF), BF16),
                pltpu.VMEM((3, OWN, 128), F32),
                pltpu.VMEM((OWN, HALF), BF16),
                pltpu.VMEM((OWN, 128), F32),
                pltpu.VMEM((2, OWN, INNER), BF16),
                pltpu.VMEM((2, ROWS, INNER), BF16),
                pltpu.VMEM((ROWS, D), BF16),
                pltpu.VMEM((OWN, D), BF16),
                pltpu.SemaphoreType.DMA((128,)),
                pltpu.SemaphoreType.DMA((128,)),
                pltpu.SemaphoreType.DMA((32,)),
            ],
            compiler_params=pltpu.CompilerParams(
                collective_id=1, has_side_effects=True, vmem_limit_bytes=60 * 2**20
            ),
            name="attend",
        )(*args)
    )


def solution(mesh):
    tokens, rows = P(("grp", "seq"), None), P("seq", None)
    in_specs = (tokens, tokens, P(), P(), P(), P(), rows, rows, rows, rows)
    return jax.shard_map(
        on_device, mesh=mesh, in_specs=in_specs, out_specs=(tokens, tokens), check_vma=False
    )
```

time: 547 us -> 134 us (0.24)
  waiting for transfers between devices: 337 us -> 0 us
  Pallas kernels: 0 us -> 129 us
  matrix products: 88 us -> 0 us
  blocking collectives: 58.5 us -> 0 us
  other arithmetic: 22.1 us -> 0 us
  local copies, waits for them, and re-layouts: 25.6 us -> 4.27 us
  between operations: 14 us -> 0.64 us
    all_gather x7 -> x0, waiting for transfers between devices: 248 us -> none  [the longest x1 57.9 us: on_device(): lax.all_gather(wq_audio, 'seq', axis=0, tiled=True)]
    pallas_call x0 -> x1, Pallas kernels: none -> 129 us  [on_device(): pl.pallas_call(attend, out_shape=[sds((ROWS, D), BF16), sds((OWN, D), BF1...]
    unnamed x11 -> x0, waiting for transfers between devices: 89.1 us -> none
    dot_general x12 -> x0, matrix products: 88 us -> none  [the longest x8 38.1 us: project(): jnp.dot(rows, weight, preferred_element_type=jnp.float32)]
    pmax x1 -> x0, blocking collectives: 58.5 us -> none  [on_device(): lax.pmax(peak_back.astype(jnp.bfloat16), 'seq').astype(peak_back.dtype)]
    reduce_sum x2 -> x0, other arithmetic: 21.9 us -> none  [the longest x1 11.3 us: on_device(): sums = jnp.sum(expo_front, axis=-1)]
    all_gather x3 -> x0, local copies, waits for them, and re-layouts: 14.1 us -> none  [the longest x1 4.73 us: on_device(): lax.all_gather(own_q, 'seq', axis=0, tiled=True)]
  transfers between devices with their start and end apart: 9 -> 0, of which waited for: 7 -> 0; matrix products, arithmetic and copies ran while one was open for 24% -> 0% of each run, Pallas kernels for 0% -> 0%
where the time goes in v2:
time: 134 us
  Pallas kernels  129 us (96%)
  local copies, waits for them, and re-layouts  4.27 us (3%)
    pallas_call x1, Pallas kernels, on_device(): pl.pallas_call(attend, out_shape=[sds((ROWS, D), BF16), sds((OWN, D), BF1...  129 us
    unnamed x2, local copies, waits for them, and re-layouts  4.27 us

profile of v2, /device:TPU:1, one launch (start us, length us, event | category | flops | bytes accessed | tf_op | source)
XLA Modules:
  0.0 134.0 jit_solution(15466462573571006307)
XLA Ops:
  0.6 129.1 %attend.1 = (bf16[512,1536]{1,0:T(8,128)(2,1)}, bf16[64,1536]{1,0:T(8,128)(2,1)}) custom-call(bf16[512,1536]{1,0:T(8,128)(2,1)} %video.1, bf16[64,1536]{1,0:T(8,128)(2,1)} %audio.1, bf16[1536,1536]{1,0:T(8,128)(2,1)} %wq.1, bf16[1536,1536]{1,0:T(8,128)(2,1)} %wk.1, bf16[1536,1536]{1,0:T(8,128)(2,1)} %wv.1, bf16[1536,1536]{1,0:T(8,128)(2,1)} %wo.1, ...), custom_call_target="tpu_custom_call" | custom-call | tf_op jit(solution)/shard_map/attend/pallas_call | solution.py:478
  129.7 2.7 %copy.14 = bf16[512,1536]{1,0:T(8,128)(2,1)} copy(bf16[512,1536]{1,0:T(8,128)(2,1)} %get-tuple-element.4) | data formatting | bytes 3145728
  132.4 1.6 %copy.15 = bf16[64,1536]{1,0:T(8,128)(2,1)} copy(bf16[64,1536]{1,0:T(8,128)(2,1)} %get-tuple-element.5) | data formatting | bytes 393216

commit v3 on v2

--- a/solution.py
+++ b/solution.py
@@ -214,6 +214,12 @@
     sqa = spread_x_then(q_a)
     arrived(sqb)
     sqb = spread_y_then(q_b)
+    swap = [sems.remote(video.at[r], vid.at[r], partner) for r in halves]
+
+    @pl.when(guest)
+    def _():
+        start(swap)
+
     arrived(sk)
     sk = spread_x_then(k_a)
     arrived(sv)
@@ -221,12 +227,6 @@
     logs[...] = jnp.zeros_like(logs)
     arrived(sqa + sqb)
     sq = spread_third(slice(0, 384))
-    swap = [sems.remote(video.at[r], vid.at[r], partner) for r in halves]
-
-    @pl.when(guest)
-    def _():
-        start(swap)
-
     arrived(a_z)
 
     slot_x = xd % 2

time: 134 us -> 144 us (1.075)
  Pallas kernels: 129 us -> 139 us
    pallas_call x1, Pallas kernels: 129 us -> 139 us  [on_device(): pl.pallas_call(attend, out_shape=[sds((ROWS, D), BF16), sds((OWN, D), BF1...]
where the time goes in v3:
time: 144 us
  Pallas kernels  139 us (97%)
  local copies, waits for them, and re-layouts  4.27 us (3%)
    pallas_call x1, Pallas kernels, on_device(): pl.pallas_call(attend, out_shape=[sds((ROWS, D), BF16), sds((OWN, D), BF1...  139 us
    unnamed x2, local copies, waits for them, and re-layouts  4.27 us

profile of v3, /device:TPU:1, one launch (start us, length us, event | category | flops | bytes accessed | tf_op | source)
XLA Modules:
  0.0 144.1 jit_solution(18271444891097191724)
XLA Ops:
  0.6 139.2 %attend.1 = (bf16[512,1536]{1,0:T(8,128)(2,1)}, bf16[64,1536]{1,0:T(8,128)(2,1)}) custom-call(bf16[512,1536]{1,0:T(8,128)(2,1)} %video.1, bf16[64,1536]{1,0:T(8,128)(2,1)} %audio.1, bf16[1536,1536]{1,0:T(8,128)(2,1)} %wq.1, bf16[1536,1536]{1,0:T(8,128)(2,1)} %wk.1, bf16[1536,1536]{1,0:T(8,128)(2,1)} %wv.1, bf16[1536,1536]{1,0:T(8,128)(2,1)} %wo.1, ...), custom_call_target="tpu_custom_call" | custom-call | tf_op jit(solution)/shard_map/attend/pallas_call | solution.py:478
  139.9 2.7 %copy.14 = bf16[512,1536]{1,0:T(8,128)(2,1)} copy(bf16[512,1536]{1,0:T(8,128)(2,1)} %get-tuple-element.4) | data formatting | bytes 3145728
  142.5 1.6 %copy.15 = bf16[64,1536]{1,0:T(8,128)(2,1)} copy(bf16[64,1536]{1,0:T(8,128)(2,1)} %get-tuple-element.5) | data formatting | bytes 393216
